TPU v7x, 32 devices: a whole 2x2x4 slice. The times are simulated.
32 devices in a mesh: parts: 2 (over x), group: 16 (over z, y, core).
Axes of the slice: x: 2, y: 2, z: 4, core: 2. Of those that a mesh axis runs over, the one named last changes fastest.
Arguments:
- tokens: bfloat16 [4096, 2560], P(('parts', 'group')), parts along dimension 0, may hold values from -6 to 6
- routes: int32 [4096, 6], P(('parts', 'group')), parts along dimension 0, may hold values from 0 to 15, as said below
- gate_quanta: int32 [4096, 6], P(('parts', 'group')), parts along dimension 0, may hold values from 1 to 65535
- gate_weight: bfloat16 [16, 2560, 768], P('group'), may hold values from -0.125 to 0.125
- up_weight: bfloat16 [16, 2560, 768], P('group'), may hold values from -0.125 to 0.125
- down_weight: bfloat16 [16, 768, 2560], P('group'), may hold values from -0.21875 to 0.21875
Outputs:
- combined: bfloat16 [4096, 2560], P(('parts', 'group')), parts along dimension 0
There are 2 independent parts, one for each index of `parts`. A program takes and returns all parts, laid end to end along the dimension named above; an argument that names none is the same for every part. Nothing has to cross between parts.
Inputs may be any that keep to these rules, and one draw needn't show every extreme that they name: `routes`: each row names 6 different experts, two in each of three of the 8 groups of 2 consecutive experts; among the rows of one device, at most 64 name experts of any one group, and some group is named by exactly 64 of them.
All inputs are finite; a program needn't handle non-finite values.
Results may differ from a plain program's by a relative error of at most 0.0057.
Values may be sent and summed in bfloat16 or wider, within the bound.
A program may use at most 64 MiB of HBM per device.

v0:
```python
import jax
import jax.numpy as jnp
from jax import lax
from jax.sharding import PartitionSpec as P


def expert_apply(received, gate_weight, up_weight, down_weight):
    senders = received.shape[0]
    slots_here = received.shape[1]
    inputs = received.reshape(senders * slots_here, received.shape[2])
    gate_part = jnp.dot(inputs, gate_weight[0], preferred_element_type=jnp.float32)
    up_part = jnp.dot(inputs, up_weight[0], preferred_element_type=jnp.float32)
    activ = (jax.nn.silu(gate_part) * up_part).astype(jnp.bfloat16)
    produced = jnp.dot(activ, down_weight[0], preferred_element_type=jnp.float32).astype(
        jnp.bfloat16
    )
    return produced.reshape(senders, slots_here, produced.shape[1])


def body(tokens, routes, gate_quanta, gate_weight, up_weight, down_weight):
    experts = lax.axis_size("group")
    tok_dev = tokens.shape[0]
    width = tokens.shape[1]
    topk = routes.shape[1]
    capacity = 4 * tok_dev * topk // (3 * experts)
    expert_ids = jnp.arange(experts, dtype=jnp.int32)
    matches = routes[:, :, None] == expert_ids[None, None, :]
    picked = jnp.sum(matches.astype(jnp.int32), axis=1)
    weight_quanta = jnp.sum(jnp.where(matches, gate_quanta[:, :, None], 0), axis=1)
    ranking = jnp.cumsum(picked, axis=0) - picked
    slot_of = jnp.where((picked == 1) & (ranking < capacity), ranking, -1)
    contract = (((0,), (0,)), ((), ()))
    selector = slot_of.T[:, None, :] == jnp.arange(capacity, dtype=jnp.int32)[None, :, None]
    selector_float = selector.astype(jnp.float32)
    selector_bf = selector.astype(jnp.bfloat16).reshape(experts * capacity, tok_dev)
    outgoing = jnp.dot(selector_bf, tokens, preferred_element_type=jnp.float32).astype(jnp.bfloat16)
    outgoing = outgoing.reshape(experts, capacity, width)
    produced = expert_apply(
        lax.all_to_all(outgoing, "group", split_axis=0, concat_axis=0, tiled=True),
        gate_weight,
        up_weight,
        down_weight,
    )
    returned = lax.all_to_all(produced, "group", split_axis=0, concat_axis=0, tiled=True)
    upper_part = (weight_quanta // 256).astype(jnp.float32).T / 256.0
    lower_part = (weight_quanta % 256).astype(jnp.float32).T / 65536.0
    combine_upper = (
        (selector_float * upper_part[:, None, :])
        .astype(jnp.bfloat16)
        .reshape(experts * capacity, tok_dev)
    )
    combine_lower = (
        (selector_float * lower_part[:, None, :])
        .astype(jnp.bfloat16)
        .reshape(experts * capacity, tok_dev)
    )
    flat_rows = returned.reshape(experts * capacity, width)
    running = lax.dot_general(
        combine_upper, flat_rows, contract, preferred_element_type=jnp.float32
    )
    running = running + lax.dot_general(
        combine_lower, flat_rows, contract, preferred_element_type=jnp.float32
    )
    return running.astype(jnp.bfloat16)


def solution(mesh):
    placed = (
        P(("parts", "group"), None),
        P(("parts", "group"), None),
        P(("parts", "group"), None),
        P("group", None, None),
        P("group", None, None),
        P("group", None, None),
    )
    return jax.shard_map(
        body, mesh=mesh, in_specs=placed, out_specs=P(("parts", "group"), None), check_vma=False
    )
```

profile of v0, /device:TPU:15, one launch (start us, length us, event | category | flops | bytes accessed | tf_op | source)
XLA Modules:
  0.0 267.0 jit_solution(3165951833706888368)
XLA Ops:
  0.0 0.0 copy-start
  0.0 0.1 eq.63
  0.1 0.8 select_reduce_fusion
  0.9 0.1 copy.20
  1.0 0.2 reduce_window_sum.11
  1.1 0.1 copy.21
  1.2 0.2 bitcast_compare_fusion
  1.4 0.0 copy-done
  1.4 1.5 convolution_convert_fusion.1
  2.9 0.0 copy-start.1
  2.9 121.3 %all_to_all.10 = bf16[16,64,2560]{2,1,0:T(8,128)(2,1)S(1)} all-to-all(bf16[16,64,2560]{2,1,0:T(8,128)(2,1)S(1)} %bitcast.66), channel_id=1, replica_groups=mesh['parts'=2,'group'=16] {'group'}, dimensions={0} | all-to-all | bytes 10485760 | tf_op jit(solution)/shard_map/all_to_all | solution.py:39
  124.3 0.0 copy-done.1
  124.3 0.0 copy-start.2
  124.3 4.2 %fusion.1 = f32[1024,768]{1,0:T(8,128)S(1)} fusion(bf16[1024,2560]{1,0:T(8,128)(2,1)S(1)} %bitcast.68, bf16[1,2560,768]{2,1,0:T(8,128)(2,1)S(1)} %copy-done.1), kind=kOutput, calls=%fused_computation.3 | convolution fusion | flops 4026531840 | bytes 12320768 | tf_op jit(solution)/shard_map/dot_general | solution.py:12
  128.5 0.0 copy-done.2
  128.5 0.0 copy-start.3
  128.5 4.5 %multiply_convert_fusion = bf16[1024,768]{1,0:T(8,128)(2,1)S(1)} fusion(f32[1024,768]{1,0:T(8,128)S(1)} %fusion.1, bf16[1024,2560]{1,0:T(8,128)(2,1)S(1)} %bitcast.69, bf16[1,2560,768]{2,1,0:T(8,128)(2,1)S(1)} %copy-done.2), kind=kOutput, calls=%fused_computation.11 | convolution fusion | flops 4031250432 | bytes 13893632 | tf_op jit(solution)/shard_map/dot_general | solution.py:11
  133.0 0.0 copy-done.3
  133.1 6.0 %convolution_convert_fusion = bf16[1024,2560]{1,0:T(8,128)(2,1)} fusion(bf16[1024,768]{1,0:T(8,128)(2,1)S(1)} %multiply_convert_fusion, bf16[1,768,2560]{2,1,0:T(8,128)(2,1)S(1)} %copy-done.3), kind=kOutput, calls=%fused_computation | convolution fusion | flops 4029153280 | bytes 10747904 | tf_op jit(solution)/shard_map/dot_general | solution.py:14
  139.1 5.4 %all-to-all-start.1 = ((bf16[16,64,2560]{2,1,0:T(8,128)(2,1)}), bf16[16,64,2560]{2,1,0:T(8,128)(2,1)}, u32[]{:S(2)}, u32[]{:S(2)}) async-start(bf16[16,64,2560]{2,1,0:T(8,128)(2,1)} %bitcast.67), calls=%async_computation.1 | async-start | bytes 10485760 | tf_op jit(solution)/shard_map/all_to_all | solution.py:44
  144.5 114.9 %all-to-all-done.1 = bf16[16,64,2560]{2,1,0:T(8,128)(2,1)} async-done(((bf16[16,64,2560]{2,1,0:T(8,128)(2,1)}), bf16[16,64,2560]{2,1,0:T(8,128)(2,1)}, u32[]{:S(2)}, u32[]{:S(2)}) %all-to-all-start.1) | async-done | bytes 5242912 | tf_op jit(solution)/shard_map/all_to_all | solution.py:44
  259.4 3.4 %convolution_bitcast_fusion = f32[128,2560]{1,0:T(8,128)S(1)} fusion(bf16[16,64,2560]{2,1,0:T(8,128)(2,1)} %all-to-all-done.1, bf16[16,128]{1,0:T(8,128)(2,1)S(1)} %get-tuple-element.8, s32[16,128]{1,0:T(8,128)S(1)} %bitcast_select_fusion), kind=kOutput, calls=%fused_computation.7 | convolution fusion | flops 671350784 | bytes 6565888 | tf_op jit(solution)/shard_map/dot_general | solution.py:61
  262.8 4.2 %fusion.6 = bf16[128,2560]{1,0:T(8,128)(2,1)} fusion(f32[128,2560]{1,0:T(8,128)S(1)} %convolution_bitcast_fusion, bf16[16,64,2560]{2,1,0:T(8,128)(2,1)} %all-to-all-done.1, bf16[16,128]{1,0:T(8,128)(2,1)S(1)} %get-tuple-element.7, s32[16,128]{1,0:T(8,128)S(1)} %bitcast_select_fusion), kind=kOutput, calls=%fused_computation.10 | convolution fusion | flops 672006144 | bytes 7221248 | tf_op jit(solution)/shard_map/dot_general | solution.py:58
  (3 shorter events, 0.0 us)
Async XLA Ops:
  0.0 1.4 copy-start
  2.9 121.3 %copy-start.1 = (bf16[1,2560,768]{2,1,0:T(8,128)(2,1)S(1)}, bf16[1,2560,768]{2,1,0:T(8,128)(2,1)}, u32[]{:S(2)}) copy-start(bf16[1,2560,768]{2,1,0:T(8,128)(2,1)} %param.10) | copy-start | bytes 11796484
  124.3 4.2 %copy-start.2 = (bf16[1,2560,768]{2,1,0:T(8,128)(2,1)S(1)}, bf16[1,2560,768]{2,1,0:T(8,128)(2,1)}, u32[]{:S(2)}) copy-start(bf16[1,2560,768]{2,1,0:T(8,128)(2,1)} %param.9) | copy-start | bytes 11796484
  128.5 4.5 %copy-start.3 = (bf16[1,768,2560]{2,1,0:T(8,128)(2,1)S(1)}, bf16[1,768,2560]{2,1,0:T(8,128)(2,1)}, u32[]{:S(2)}) copy-start(bf16[1,768,2560]{2,1,0:T(8,128)(2,1)} %param.11) | copy-start | bytes 11796484
  139.1 120.3 %all-to-all-start.1 = ((bf16[16,64,2560]{2,1,0:T(8,128)(2,1)}), bf16[16,64,2560]{2,1,0:T(8,128)(2,1)}, u32[]{:S(2)}, u32[]{:S(2)}) async-start(bf16[16,64,2560]{2,1,0:T(8,128)(2,1)} %bitcast.67), calls=%async_computation.1 | async-start | bytes 10485760 | tf_op jit(solution)/shard_map/all_to_all | solution.py:44
where the time goes:
time: 267 us
  blocking collectives  121 us (45%)
  waiting for transfers between devices  115 us (43%)
  matrix products  23.8 us (9%)
  starting transfers between devices  5.39 us (2%)
    all_to_all x1, blocking collectives, body(): lax.all_to_all(outgoing, 'group', split_axis=0, concat_axis=0, tiled=True)  121 us
    all_to_all x1, waiting for transfers between devices, body(): lax.all_to_all(produced, 'group', split_axis=0, concat_axis=0, tiled=True)  115 us
    dot_general x1, matrix products, expert_apply(): jnp.dot(activ, down_weight[0], preferred_element_type=jnp.float32)  6.03 us
    all_to_all x1, starting transfers between devices, body(): lax.all_to_all(produced, 'group', split_axis=0, concat_axis=0, tiled=True)  5.39 us
  transfers between devices with their start and end apart: 1, of which 1 were waited for; matrix products, arithmetic and copies ran while one was open for 0% of the time, Pallas kernels for 0%

commit v1 on v0

--- a/solution.py
+++ b/solution.py
@@ -1,7 +1,265 @@
 import jax
 import jax.numpy as jnp
 from jax import lax
+from jax.experimental import pallas as pl
+from jax.experimental.pallas import tpu as pltpu
 from jax.sharding import PartitionSpec as P
+
+MESH = pl.DeviceIdType.MESH
+CHIPS = 8
+EXTRA = 128
+
+
+def flip(chip, k):
+    low = lax.rem(chip + k, 2)
+    mid = lax.rem(chip // 2 + k // 2, 2)
+    high = lax.rem(chip // 4 + k // 4, 2)
+    return high * 4 + mid * 2 + low
+
+
+def paired_kernel(
+    tok_ref, routes_ref, quanta_ref, gw_hbm, uw_hbm, dw_hbm, out_ref,
+    gw, uw, dw, ext, slot_t, sel, outgoing, recv, activ, weight, contrib, sib, total, ret,
+    w_sem, send1, recv1, send2, recv2, send3, recv3, send4, recv4,
+):
+    part = lax.axis_index("parts")
+    me = lax.axis_index("group")
+    chip, core = me // 2, lax.rem(me, 2)
+    other = 1 - core
+    sibling = (part, chip * 2 + other)
+    tok_dev, width = tok_ref.shape
+    cap = sel.shape[1]
+    hid = gw.shape[1]
+
+    loads = [
+        pltpu.make_async_copy(gw_hbm.at[0], gw, w_sem.at[0]),
+        pltpu.make_async_copy(uw_hbm.at[0], uw, w_sem.at[1]),
+        pltpu.make_async_copy(dw_hbm.at[0], dw, w_sem.at[2]),
+    ]
+    for load in loads:
+        load.start()
+
+    barrier = pltpu.get_barrier_semaphore()
+    for k in range(1, CHIPS):
+        pl.semaphore_signal(
+            barrier, inc=1, device_id=(part, flip(chip, k) * 2 + core), device_id_type=MESH
+        )
+    pl.semaphore_signal(barrier, inc=1, device_id=sibling, device_id_type=MESH)
+
+    lanes = lax.broadcasted_iota(jnp.int32, (tok_dev, 128), 1)
+    picked = jnp.zeros((tok_dev, 128), jnp.float32)
+    quanta = jnp.zeros((tok_dev, 128), jnp.int32)
+    for k in range(routes_ref.shape[1]):
+        route = routes_ref[:, k : k + 1]
+        picked += (route == lanes).astype(jnp.float32)
+        quanta += jnp.where(
+            (route == lanes) | (route == lanes - 16), quanta_ref[:, k : k + 1], 0
+        )
+    upper = (quanta // 256).astype(jnp.float32) / 256.0
+    lower = (quanta % 256).astype(jnp.float32) / 65536.0
+    ext[:, :width] = tok_ref[...]
+    ext[:, width:] = jnp.where(lanes < 16, upper, lower).astype(jnp.bfloat16)
+    before = (lax.broadcasted_iota(jnp.int32, (tok_dev, tok_dev), 1)
+              < lax.broadcasted_iota(jnp.int32, (tok_dev, tok_dev), 0))
+    ranking = jnp.dot(
+        before.astype(jnp.bfloat16), picked.astype(jnp.bfloat16),
+        preferred_element_type=jnp.float32,
+    )
+    slot_t[...] = jnp.where(picked > 0.5, ranking, -1.0).T
+    slot_ids = lax.broadcasted_iota(jnp.int32, (cap, tok_dev), 0).astype(jnp.float32)
+
+    pl.semaphore_wait(barrier, CHIPS)
+
+    def first(k):
+        return pltpu.make_async_remote_copy(
+            src_ref=outgoing.at[k], dst_ref=recv.at[k, core],
+            send_sem=send1.at[k], recv_sem=recv1.at[k],
+            device_id=(part, flip(chip, k) * 2 + core), device_id_type=MESH)
+
+    def share_from(src, k):
+        return pltpu.make_async_remote_copy(
+            src_ref=src, dst_ref=recv.at[k, core],
+            send_sem=send2.at[k], recv_sem=recv2.at[k],
+            device_id=sibling, device_id_type=MESH)
+
+    def share(k):
+        return share_from(recv.at[k, core], k)
+
+    def share_in(k):
+        return pltpu.make_async_remote_copy(
+            src_ref=recv.at[k, other], dst_ref=recv.at[k, other],
+            send_sem=send2.at[k], recv_sem=recv2.at[k],
+            device_id=sibling, device_id_type=MESH)
+
+    def cross(k):
+        return pltpu.make_async_remote_copy(
+            src_ref=contrib.at[k, other], dst_ref=sib.at[k],
+            send_sem=send3.at[k], recv_sem=recv3.at[k],
+            device_id=sibling, device_id_type=MESH)
+
+    def back(k):
+        return pltpu.make_async_remote_copy(
+            src_ref=total.at[k], dst_ref=ret.at[k],
+            send_sem=send4.at[k], recv_sem=recv4.at[k],
+            device_id=(part, flip(chip, k) * 2 + core), device_id_type=MESH)
+
+    def pick_rows(k):
+        dest = flip(chip, k)
+        chosen = (slot_t[pl.ds(2 * dest, 1), :] == slot_ids).astype(jnp.float32)
+        sel[k] = chosen
+        return jnp.dot(
+            chosen.astype(jnp.bfloat16), ext[...], preferred_element_type=jnp.float32
+        ).astype(jnp.bfloat16)
+
+    def dispatch(j, carry):
+        k = CHIPS - 1 - j
+        outgoing[k] = pick_rows(k)
+        first(k).start()
+        return carry
+
+    lax.fori_loop(0, CHIPS - 1, dispatch, 0)
+    recv[0, core] = pick_rows(0)
+    share(0).start()
+    for load in loads:
+        load.wait()
+
+    rows = 4 * cap
+    lane_ids = lax.broadcasted_iota(jnp.int32, (rows, EXTRA), 1)
+
+    def expert(j, carry):
+        pair = CHIPS // 2 - 1 - j
+        base = 2 * pair
+
+        def forward(k):
+            first(k).wait_recv()
+            share(k).start()
+
+        forward(base + 1)
+
+        @pl.when(base > 0)
+        def _():
+            forward(base)
+
+        share_in(base + 1).wait_recv()
+        share_in(base).wait_recv()
+
+        def hidden(t, c):
+            cols = pl.ds(pl.multiple_of(t * 256, 256), 256)
+            x = recv[pl.ds(base, 2), :, :, :width].reshape(rows, width)
+            g = jnp.dot(x, gw[:, cols], preferred_element_type=jnp.float32)
+            u = jnp.dot(x, uw[:, cols], preferred_element_type=jnp.float32)
+            activ[:, cols] = (g / (1.0 + jnp.exp(-g)) * u).astype(jnp.bfloat16)
+            return c
+
+        lax.fori_loop(0, hid // 256, hidden, 0)
+        marks = recv[pl.ds(base, 2), :, :, width:].reshape(rows, EXTRA).astype(jnp.float32)
+        mine = (lane_ids == me) | (lane_ids == me + 16)
+        weight[...] = jnp.broadcast_to(
+            jnp.sum(jnp.where(mine, marks, 0.0), axis=1, keepdims=True), (rows, 128))
+
+        def down(t, c):
+            cols = pl.ds(pl.multiple_of(t * 512, 512), 512)
+            o = jnp.dot(activ[...], dw[:, cols], preferred_element_type=jnp.float32)
+            o = o * weight[:, :1]
+            contrib[pl.ds(base, 2), :, :, cols] = o.astype(jnp.bfloat16).reshape(2, 2, cap, 512)
+            return c
+
+        lax.fori_loop(0, width // 512, down, 0)
+        cross(base + 1).start()
+        cross(base).start()
+
+        def finish(k):
+            cross(k).wait_recv()
+            return (
+                contrib[k, core].astype(jnp.float32) + sib[k].astype(jnp.float32)
+            ).astype(jnp.bfloat16)
+
+        total[base + 1] = finish(base + 1)
+        back(base + 1).start()
+
+        @pl.when(base > 0)
+        def _():
+            total[base] = finish(base)
+            back(base).start()
+
+        @pl.when(base == 0)
+        def _():
+            ret[0] = finish(0)
+
+        return carry
+
+    lax.fori_loop(0, CHIPS // 2, expert, 0)
+
+    def arrive(j, carry):
+        back(CHIPS - 1 - j).wait_recv()
+        return carry
+
+    lax.fori_loop(0, CHIPS - 1, arrive, 0)
+    spread = sel[...].reshape(CHIPS * cap, tok_dev).T.astype(jnp.bfloat16)
+
+    def gather(t, c):
+        cols = pl.ds(pl.multiple_of(t * 512, 512), 512)
+        got = ret[:, :, cols].reshape(CHIPS * cap, 512)
+        out_ref[:, cols] = jnp.dot(
+            spread, got, preferred_element_type=jnp.float32
+        ).astype(out_ref.dtype)
+        return c
+
+    lax.fori_loop(0, width // 512, gather, 0)
+
+    def drain(k, carry):
+        first(k).wait_send()
+        back(k).wait_send()
+        return carry
+
+    lax.fori_loop(1, CHIPS, drain, 0)
+
+    def drain_sibling(k, carry):
+        share(k).wait_send()
+        cross(k).wait_send()
+        return carry
+
+    lax.fori_loop(0, CHIPS, drain_sibling, 0)
+
+
+def paired_body(tokens, routes, gate_quanta, gate_weight, up_weight, down_weight):
+    tok_dev, width = tokens.shape
+    experts = lax.axis_size("group")
+    cap = 4 * tok_dev * routes.shape[1] // (3 * experts)
+    hid = gate_weight.shape[2]
+    bf, f32 = jnp.bfloat16, jnp.float32
+    dma = pltpu.SemaphoreType.DMA
+    vmem = pl.BlockSpec(memory_space=pltpu.VMEM)
+    hbm = pl.BlockSpec(memory_space=pl.ANY)
+    return pl.pallas_call(
+        paired_kernel,
+        out_shape=jax.ShapeDtypeStruct((tok_dev, width), bf),
+        in_specs=[vmem, vmem, vmem, hbm, hbm, hbm],
+        out_specs=vmem,
+        scratch_shapes=[
+            pltpu.VMEM((width, hid), bf),
+            pltpu.VMEM((width, hid), bf),
+            pltpu.VMEM((hid, width), bf),
+            pltpu.VMEM((tok_dev, width + EXTRA), bf),
+            pltpu.VMEM((128, tok_dev), f32),
+            pltpu.VMEM((CHIPS, cap, tok_dev), f32),
+            pltpu.VMEM((CHIPS, cap, width + EXTRA), bf),
+            pltpu.VMEM((CHIPS, 2, cap, width + EXTRA), bf),
+            pltpu.VMEM((4 * cap, hid), bf),
+            pltpu.VMEM((4 * cap, 128), f32),
+            pltpu.VMEM((CHIPS, 2, cap, width), bf),
+            pltpu.VMEM((CHIPS, cap, width), bf),
+            pltpu.VMEM((CHIPS, cap, width), bf),
+            pltpu.VMEM((CHIPS, cap, width), bf),
+            dma((3,)),
+        ] + [dma((CHIPS,))] * 8,
+        compiler_params=pltpu.CompilerParams(
+            collective_id=0, has_side_effects=True, vmem_limit_bytes=52 * 1024 * 1024
+        ),
+        cost_estimate=pl.CostEstimate(
+            flops=6 * 16 * cap * width * hid, bytes_accessed=6 * width * hid, transcendentals=0
+        ),
+    )(tokens, routes, gate_quanta, gate_weight, up_weight, down_weight)
 
 
 def expert_apply(received, gate_weight, up_weight, down_weight):
@@ -73,6 +331,7 @@
         P("group", None, None),
         P("group", None, None),
     )
+    chosen = paired_body if mesh.shape["group"] == 2 * CHIPS else body
     return jax.shard_map(
-        body, mesh=mesh, in_specs=placed, out_specs=P(("parts", "group"), None), check_vma=False
-    )
+        chosen, mesh=mesh, in_specs=placed, out_specs=P(("parts", "group"), None), check_vma=False
+    )

time: 267 us -> 133 us (0.50)
  the two profiles are of different devices: /device:TPU:15 before, /device:TPU:0 now
where the time goes in v1:
time: 133 us
  Pallas kernels  129 us (97%)
  local copies, waits for them, and re-layouts  3.51 us (3%)
    pallas_call x1, Pallas kernels, paired_body(): pl.pallas_call(paired_kernel, out_shape=jax.ShapeDtypeStruct((tok_dev, wi...  129 us
    unnamed x5, local copies, waits for them, and re-layouts  3.51 us

profile of v1, /device:TPU:0, one launch (start us, length us, event | category | flops | bytes accessed | tf_op | source)
XLA Modules:
  0.0 132.7 jit_solution(1892380408223342963)
XLA Ops:
  0.0 0.8 copy.7.routes_ref
  0.8 0.8 copy.8.quanta_ref
  1.6 0.0 copy-start
  1.6 1.1 copy-done
  2.7 129.2 %shard_map.64 = bf16[128,2560]{1,0:T(8,128)(2,1)S(1)} custom-call(bf16[128,2560]{1,0:T(8,128)(2,1)S(1)} %copy-done, s32[128,6]{1,0:T(8,128)S(1)} %copy.7.routes_ref, s32[128,6]{1,0:T(8,128)S(1)} %copy.8.quanta_ref, bf16[1,2560,768]{2,1,0:T(8,128)(2,1)} %gw_hbm.1, bf16[1,2560,768]{2,1,0:T(8,128)(2,1)} %uw_hbm.1, bf16[1,768,2560]{2,1,0:T(8,128)(2,1)} %dw_hbm.1), custom_call_target="tpu_custom_call" | custom-call | flops 12079595520 | bytes 11796480 | tf_op jit(solution)/shard_map/pallas_call | solution.py:234
  131.9 0.8 copy.10
Async XLA Ops:
  1.6 1.1 copy-start

commit v2 on v1

--- a/solution.py
+++ b/solution.py
@@ -7,6 +7,7 @@
 
 MESH = pl.DeviceIdType.MESH
 CHIPS = 8
+HALF = CHIPS // 2
 EXTRA = 128
 
 
@@ -20,7 +21,7 @@
 def paired_kernel(
     tok_ref, routes_ref, quanta_ref, gw_hbm, uw_hbm, dw_hbm, out_ref,
     gw, uw, dw, ext, slot_t, sel, outgoing, recv, activ, weight, contrib, sib, total, ret,
-    w_sem, send1, recv1, send2, recv2, send3, recv3, send4, recv4,
+    partial, landed, w_sem, block_send, block_recv, part_send, part_recv, send1, recv1, send2, recv2, send3, recv3, send4, recv4,
 ):
     part = lax.axis_index("parts")
     me = lax.axis_index("group")
@@ -40,7 +41,7 @@
         load.start()
 
     barrier = pltpu.get_barrier_semaphore()
-    for k in range(1, CHIPS):
+    for k in range(1, HALF + 1):
         pl.semaphore_signal(
             barrier, inc=1, device_id=(part, flip(chip, k) * 2 + core), device_id_type=MESH
         )
@@ -57,24 +58,34 @@
         )
     upper = (quanta // 256).astype(jnp.float32) / 256.0
     lower = (quanta % 256).astype(jnp.float32) / 65536.0
-    ext[:, :width] = tok_ref[...]
-    ext[:, width:] = jnp.where(lanes < 16, upper, lower).astype(jnp.bfloat16)
     before = (lax.broadcasted_iota(jnp.int32, (tok_dev, tok_dev), 1)
               < lax.broadcasted_iota(jnp.int32, (tok_dev, tok_dev), 0))
     ranking = jnp.dot(
         before.astype(jnp.bfloat16), picked.astype(jnp.bfloat16),
         preferred_element_type=jnp.float32,
     )
-    slot_t[...] = jnp.where(picked > 0.5, ranking, -1.0).T
+    slots = jnp.where(picked > 0.5, ranking, -1.0)
+    slot_t[0] = slots.T
+    ext[0, :, :width] = tok_ref[...]
+    marks = jnp.where(lanes < 16, upper, lower)
+    ext[0, :, width : width + EXTRA] = marks.astype(jnp.bfloat16)
+    ext[0, :, width + EXTRA :] = slots.astype(jnp.bfloat16)
     slot_ids = lax.broadcasted_iota(jnp.int32, (cap, tok_dev), 0).astype(jnp.float32)
 
-    pl.semaphore_wait(barrier, CHIPS)
+    pl.semaphore_wait(barrier, HALF + 1)
+
+    mirror = (part, flip(chip, HALF) * 2 + core)
+    block = pltpu.make_async_remote_copy(
+        src_ref=ext.at[0], dst_ref=ext.at[1],
+        send_sem=block_send.at[0], recv_sem=block_recv.at[0],
+        device_id=mirror, device_id_type=MESH)
+    block.start()
 
     def first(k):
         return pltpu.make_async_remote_copy(
             src_ref=outgoing.at[k], dst_ref=recv.at[k, core],
             send_sem=send1.at[k], recv_sem=recv1.at[k],
-            device_id=(part, flip(chip, k) * 2 + core), device_id_type=MESH)
+            device_id=(part, flip(chip, lax.rem(k, HALF)) * 2 + core), device_id_type=MESH)
 
     def share_from(src, k):
         return pltpu.make_async_remote_copy(
@@ -101,23 +112,30 @@
         return pltpu.make_async_remote_copy(
             src_ref=total.at[k], dst_ref=ret.at[k],
             send_sem=send4.at[k], recv_sem=recv4.at[k],
-            device_id=(part, flip(chip, k) * 2 + core), device_id_type=MESH)
+            device_id=(part, flip(chip, lax.rem(k, HALF)) * 2 + core), device_id_type=MESH)
+
+    def sum_piece(h):
+        return pltpu.make_async_remote_copy(
+            src_ref=partial.at[h], dst_ref=landed.at[h],
+            send_sem=part_send.at[h], recv_sem=part_recv.at[h],
+            device_id=mirror, device_id_type=MESH)
 
     def pick_rows(k):
-        dest = flip(chip, k)
-        chosen = (slot_t[pl.ds(2 * dest, 1), :] == slot_ids).astype(jnp.float32)
+        dest = flip(chip, lax.rem(k, HALF))
+        held = k // HALF
+        chosen = (slot_t[held, pl.ds(2 * dest, 1), :] == slot_ids).astype(jnp.float32)
         sel[k] = chosen
         return jnp.dot(
-            chosen.astype(jnp.bfloat16), ext[...], preferred_element_type=jnp.float32
+            chosen.astype(jnp.bfloat16), ext[held, :, : width + EXTRA],
+            preferred_element_type=jnp.float32,
         ).astype(jnp.bfloat16)
 
-    def dispatch(j, carry):
-        k = CHIPS - 1 - j
+    def dispatch(k, carry):
         outgoing[k] = pick_rows(k)
         first(k).start()
         return carry
 
-    lax.fori_loop(0, CHIPS - 1, dispatch, 0)
+    lax.fori_loop(1, HALF, dispatch, 0)
     recv[0, core] = pick_rows(0)
     share(0).start()
     for load in loads:
@@ -126,9 +144,9 @@
     rows = 4 * cap
     lane_ids = lax.broadcasted_iota(jnp.int32, (rows, EXTRA), 1)
 
-    def expert(j, carry):
-        pair = CHIPS // 2 - 1 - j
+    def expert(pair, far):
         base = 2 * pair
+        local = 4 if far else 0
 
         def forward(k):
             first(k).wait_recv()
@@ -136,7 +154,7 @@
 
         forward(base + 1)
 
-        @pl.when(base > 0)
+        @pl.when(base != local)
         def _():
             forward(base)
 
@@ -175,44 +193,94 @@
             ).astype(jnp.bfloat16)
 
         total[base + 1] = finish(base + 1)
-        back(base + 1).start()
-
-        @pl.when(base > 0)
+        if far:
+            back(base + 1).start()
+
+        @pl.when(base != local)
         def _():
             total[base] = finish(base)
-            back(base).start()
-
-        @pl.when(base == 0)
+            if far:
+                back(base).start()
+
+        @pl.when(base == local)
         def _():
-            ret[0] = finish(0)
-
-        return carry
-
-    lax.fori_loop(0, CHIPS // 2, expert, 0)
-
-    def arrive(j, carry):
-        back(CHIPS - 1 - j).wait_recv()
-        return carry
-
-    lax.fori_loop(0, CHIPS - 1, arrive, 0)
-    spread = sel[...].reshape(CHIPS * cap, tok_dev).T.astype(jnp.bfloat16)
-
-    def gather(t, c):
-        cols = pl.ds(pl.multiple_of(t * 512, 512), 512)
-        got = ret[:, :, cols].reshape(CHIPS * cap, 512)
-        out_ref[:, cols] = jnp.dot(
-            spread, got, preferred_element_type=jnp.float32
-        ).astype(out_ref.dtype)
-        return c
-
-    lax.fori_loop(0, width // 512, gather, 0)
+            ret[local] = finish(local)
+
+    def near_pair(pair, carry):
+        expert(pair, False)
+        return carry
+
+    def far_pair(pair, carry):
+        expert(pair, True)
+        return carry
+
+    lax.fori_loop(0, 2, near_pair, 0)
+
+    block.wait_recv()
+    slot_t[1] = ext[1, :, width + EXTRA :].astype(jnp.float32).T
+    lax.fori_loop(HALF + 1, CHIPS, dispatch, 0)
+    recv[HALF, core] = pick_rows(HALF)
+    share(HALF).start()
+    lax.fori_loop(2, 4, far_pair, 0)
+
+    def arrive(k, carry):
+        back(k).wait_recv()
+        return carry
+
+    def send_back(k, carry):
+        back(k).start()
+        return carry
+
+    half_width = width // 2
+    span = half_width // 5
+
+    def spread_of(lo):
+        return sel[lo : lo + HALF].reshape(HALF * cap, tok_dev).T.astype(jnp.bfloat16)
+
+    lax.fori_loop(HALF + 1, CHIPS, arrive, 0)
+    spread_far = spread_of(HALF)
+    for h in range(2):
+        def add_far(t, c):
+            cols = pl.ds(pl.multiple_of(h * half_width + t * span, span), span)
+            got = ret[HALF:, :, cols].reshape(HALF * cap, span)
+            into = pl.ds(pl.multiple_of(t * span, span), span)
+            partial[h, :, into] = jnp.dot(
+                spread_far, got, preferred_element_type=jnp.float32
+            ).astype(jnp.bfloat16)
+            return c
+
+        lax.fori_loop(0, 5, add_far, 0)
+        sum_piece(h).start()
+
+    lax.fori_loop(1, HALF, send_back, 0)
+    lax.fori_loop(1, HALF, arrive, 0)
+    spread_near = spread_of(0)
+    for h in range(2):
+        sum_piece(h).wait_recv()
+
+        def gather(t, c):
+            cols = pl.ds(pl.multiple_of(h * half_width + t * span, span), span)
+            got = ret[:HALF, :, cols].reshape(HALF * cap, span)
+            from_far = landed[h, :, pl.ds(pl.multiple_of(t * span, span), span)]
+            out_ref[:, cols] = (
+                jnp.dot(spread_near, got, preferred_element_type=jnp.float32)
+                + from_far.astype(jnp.float32)
+            ).astype(out_ref.dtype)
+            return c
+
+        lax.fori_loop(0, 5, gather, 0)
+
+    block.wait_send()
+    for h in range(2):
+        sum_piece(h).wait_send()
 
     def drain(k, carry):
         first(k).wait_send()
         back(k).wait_send()
         return carry
 
-    lax.fori_loop(1, CHIPS, drain, 0)
+    lax.fori_loop(1, HALF, drain, 0)
+    lax.fori_loop(HALF + 1, CHIPS, drain, 0)
 
     def drain_sibling(k, carry):
         share(k).wait_send()
@@ -240,8 +308,8 @@
             pltpu.VMEM((width, hid), bf),
             pltpu.VMEM((width, hid), bf),
             pltpu.VMEM((hid, width), bf),
-            pltpu.VMEM((tok_dev, width + EXTRA), bf),
-            pltpu.VMEM((128, tok_dev), f32),
+            pltpu.VMEM((2, tok_dev, width + 2 * EXTRA), bf),
+            pltpu.VMEM((2, 128, tok_dev), f32),
             pltpu.VMEM((CHIPS, cap, tok_dev), f32),
             pltpu.VMEM((CHIPS, cap, width + EXTRA), bf),
             pltpu.VMEM((CHIPS, 2, cap, width + EXTRA), bf),
@@ -251,7 +319,10 @@
             pltpu.VMEM((CHIPS, cap, width), bf),
             pltpu.VMEM((CHIPS, cap, width), bf),
             pltpu.VMEM((CHIPS, cap, width), bf),
+            pltpu.VMEM((2, tok_dev, width // 2), bf),
+            pltpu.VMEM((2, tok_dev, width // 2), bf),
             dma((3,)),
+            dma((1,)), dma((1,)), dma((2,)), dma((2,)),
         ] + [dma((CHIPS,))] * 8,
         compiler_params=pltpu.CompilerParams(
             collective_id=0, has_side_effects=True, vmem_limit_bytes=52 * 1024 * 1024

time: 133 us -> 141 us (1.060)
  the two profiles are of different devices: /device:TPU:0 before, /device:TPU:16 now
where the time goes in v2:
time: 141 us; the launch traced here: 140 us
  Pallas kernels  137 us (97%)
  local copies, waits for them, and re-layouts  3.51 us (2%)
    pallas_call x1, Pallas kernels, paired_body(): pl.pallas_call(paired_kernel, out_shape=jax.ShapeDtypeStruct((tok_dev, wi...  137 us
    unnamed x5, local copies, waits for them, and re-layouts  3.51 us

profile of v2, /device:TPU:16, one launch (start us, length us, event | category | flops | bytes accessed | tf_op | source)
XLA Modules:
  0.0 140.3 jit_solution(11993293600500990310)
XLA Ops:
  0.0 0.8 copy.7.routes_ref
  0.8 0.8 copy.8.quanta_ref
  1.6 0.0 copy-start
  1.6 1.1 copy-done
  2.7 136.8 %shard_map.64 = bf16[128,2560]{1,0:T(8,128)(2,1)S(1)} custom-call(bf16[128,2560]{1,0:T(8,128)(2,1)S(1)} %copy-done, s32[128,6]{1,0:T(8,128)S(1)} %copy.7.routes_ref, s32[128,6]{1,0:T(8,128)S(1)} %copy.8.quanta_ref, bf16[1,2560,768]{2,1,0:T(8,128)(2,1)} %gw_hbm.1, bf16[1,2560,768]{2,1,0:T(8,128)(2,1)} %uw_hbm.1, bf16[1,768,2560]{2,1,0:T(8,128)(2,1)} %dw_hbm.1), custom_call_target="tpu_custom_call" | custom-call | flops 12079595520 | bytes 11796480 | tf_op jit(solution)/shard_map/pallas_call | solution.py:302
  139.5 0.8 copy.10
Async XLA Ops:
  1.6 1.1 copy-start

commit v3 on v2

--- a/solution.py
+++ b/solution.py
@@ -138,9 +138,6 @@
     lax.fori_loop(1, HALF, dispatch, 0)
     recv[0, core] = pick_rows(0)
     share(0).start()
-    for load in loads:
-        load.wait()
-
     rows = 4 * cap
     lane_ids = lax.broadcasted_iota(jnp.int32, (rows, EXTRA), 1)
 
@@ -185,26 +182,24 @@
         lax.fori_loop(0, width // 512, down, 0)
         cross(base + 1).start()
         cross(base).start()
-
-        def finish(k):
-            cross(k).wait_recv()
-            return (
-                contrib[k, core].astype(jnp.float32) + sib[k].astype(jnp.float32)
-            ).astype(jnp.bfloat16)
-
-        total[base + 1] = finish(base + 1)
         if far:
-            back(base + 1).start()
-
-        @pl.when(base != local)
+            finish(base + 1)
+            finish(base)
+
+    def finish(k):
+        cross(k).wait_recv()
+        both = (
+            contrib[k, core].astype(jnp.float32) + sib[k].astype(jnp.float32)
+        ).astype(jnp.bfloat16)
+
+        @pl.when(lax.rem(k, HALF) != 0)
         def _():
-            total[base] = finish(base)
-            if far:
-                back(base).start()
-
-        @pl.when(base == local)
+            total[k] = both
+            back(k).start()
+
+        @pl.when(lax.rem(k, HALF) == 0)
         def _():
-            ret[local] = finish(local)
+            ret[k] = both
 
     def near_pair(pair, carry):
         expert(pair, False)
@@ -213,14 +208,15 @@
     def far_pair(pair, carry):
         expert(pair, True)
         return carry
-
-    lax.fori_loop(0, 2, near_pair, 0)
 
     block.wait_recv()
     slot_t[1] = ext[1, :, width + EXTRA :].astype(jnp.float32).T
     lax.fori_loop(HALF + 1, CHIPS, dispatch, 0)
     recv[HALF, core] = pick_rows(HALF)
     share(HALF).start()
+    for load in loads:
+        load.wait()
+    lax.fori_loop(0, 2, near_pair, 0)
     lax.fori_loop(2, 4, far_pair, 0)
 
     def arrive(k, carry):
@@ -228,7 +224,7 @@
         return carry
 
     def send_back(k, carry):
-        back(k).start()
+        finish(k)
         return carry
 
     half_width = width // 2
@@ -252,7 +248,7 @@
         lax.fori_loop(0, 5, add_far, 0)
         sum_piece(h).start()
 
-    lax.fori_loop(1, HALF, send_back, 0)
+    lax.fori_loop(0, HALF, send_back, 0)
     lax.fori_loop(1, HALF, arrive, 0)
     spread_near = spread_of(0)
     for h in range(2):

time: 141 us -> 124 us (0.88)
  the two profiles are of different devices: /device:TPU:16 before, /device:TPU:0 now
where the time goes in v3:
time: 124 us
  Pallas kernels  120 us (97%)
  local copies, waits for them, and re-layouts  3.51 us (3%)
    pallas_call x1, Pallas kernels, paired_body(): pl.pallas_call(paired_kernel, out_shape=jax.ShapeDtypeStruct((tok_dev, wi...  120 us
    unnamed x5, local copies, waits for them, and re-layouts  3.51 us

profile of v3, /device:TPU:0, one launch (start us, length us, event | category | flops | bytes accessed | tf_op | source)
XLA Modules:
  0.0 123.6 jit_solution(3046490173664684335)
XLA Ops:
  0.0 0.8 copy.7.routes_ref
  0.8 0.8 copy.8.quanta_ref
  1.6 0.0 copy-start
  1.6 1.1 copy-done
  2.7 120.0 %shard_map.64 = bf16[128,2560]{1,0:T(8,128)(2,1)S(1)} custom-call(bf16[128,2560]{1,0:T(8,128)(2,1)S(1)} %copy-done, s32[128,6]{1,0:T(8,128)S(1)} %copy.7.routes_ref, s32[128,6]{1,0:T(8,128)S(1)} %copy.8.quanta_ref, bf16[1,2560,768]{2,1,0:T(8,128)(2,1)} %gw_hbm.1, bf16[1,2560,768]{2,1,0:T(8,128)(2,1)} %uw_hbm.1, bf16[1,768,2560]{2,1,0:T(8,128)(2,1)} %dw_hbm.1), custom_call_target="tpu_custom_call" | custom-call | flops 12079595520 | bytes 11796480 | tf_op jit(solution)/shard_map/pallas_call | solution.py:298
  122.7 0.8 copy.10
Async XLA Ops:
  1.6 1.1 copy-start

commit v4 on v3

--- a/solution.py
+++ b/solution.py
@@ -108,10 +108,11 @@
             send_sem=send3.at[k], recv_sem=recv3.at[k],
             device_id=sibling, device_id_type=MESH)
 
-    def back(k):
-        return pltpu.make_async_remote_copy(
-            src_ref=total.at[k], dst_ref=ret.at[k],
-            send_sem=send4.at[k], recv_sem=recv4.at[k],
+    def back(h, k):
+        cols = pl.ds(h * (width // 2), width // 2)
+        return pltpu.make_async_remote_copy(
+            src_ref=total.at[k, :, cols], dst_ref=ret.at[k, :, cols],
+            send_sem=send4.at[h, k], recv_sem=recv4.at[h, k],
             device_id=(part, flip(chip, lax.rem(k, HALF)) * 2 + core), device_id_type=MESH)
 
     def sum_piece(h):
@@ -183,8 +184,17 @@
         cross(base + 1).start()
         cross(base).start()
         if far:
-            finish(base + 1)
-            finish(base)
+            finish_pair(base)
+
+    def finish_pair(base):
+        finish(base + 1)
+        finish(base)
+        for h in range(2):
+            back(h, base + 1).start()
+
+            @pl.when(lax.rem(base, HALF) != 0)
+            def _():
+                back(h, base).start()
 
     def finish(k):
         cross(k).wait_recv()
@@ -195,7 +205,6 @@
         @pl.when(lax.rem(k, HALF) != 0)
         def _():
             total[k] = both
-            back(k).start()
 
         @pl.when(lax.rem(k, HALF) == 0)
         def _():
@@ -217,15 +226,16 @@
     for load in loads:
         load.wait()
     lax.fori_loop(0, 2, near_pair, 0)
+    for pair in range(2):
+        finish_pair(2 * pair)
     lax.fori_loop(2, 4, far_pair, 0)
 
-    def arrive(k, carry):
-        back(k).wait_recv()
-        return carry
-
-    def send_back(k, carry):
-        finish(k)
-        return carry
+    def arrive(h):
+        def one(k, carry):
+            back(h, k).wait_recv()
+            return carry
+
+        return one
 
     half_width = width // 2
     span = half_width // 5
@@ -233,9 +243,10 @@
     def spread_of(lo):
         return sel[lo : lo + HALF].reshape(HALF * cap, tok_dev).T.astype(jnp.bfloat16)
 
-    lax.fori_loop(HALF + 1, CHIPS, arrive, 0)
     spread_far = spread_of(HALF)
     for h in range(2):
+        lax.fori_loop(HALF + 1, CHIPS, arrive(h), 0)
+
         def add_far(t, c):
             cols = pl.ds(pl.multiple_of(h * half_width + t * span, span), span)
             got = ret[HALF:, :, cols].reshape(HALF * cap, span)
@@ -248,8 +259,8 @@
         lax.fori_loop(0, 5, add_far, 0)
         sum_piece(h).start()
 
-    lax.fori_loop(0, HALF, send_back, 0)
-    lax.fori_loop(1, HALF, arrive, 0)
+    for h in range(2):
+        lax.fori_loop(1, HALF, arrive(h), 0)
     spread_near = spread_of(0)
     for h in range(2):
         sum_piece(h).wait_recv()
@@ -272,7 +283,8 @@
 
     def drain(k, carry):
         first(k).wait_send()
-        back(k).wait_send()
+        back(0, k).wait_send()
+        back(1, k).wait_send()
         return carry
 
     lax.fori_loop(1, HALF, drain, 0)
@@ -319,7 +331,7 @@
             pltpu.VMEM((2, tok_dev, width // 2), bf),
             dma((3,)),
             dma((1,)), dma((1,)), dma((2,)), dma((2,)),
-        ] + [dma((CHIPS,))] * 8,
+        ] + [dma((CHIPS,))] * 6 + [dma((2, CHIPS))] * 2,
         compiler_params=pltpu.CompilerParams(
             collective_id=0, has_side_effects=True, vmem_limit_bytes=52 * 1024 * 1024
         ),

time: 124 us -> 119 us (0.960)
  Pallas kernels: 120 us -> 115 us
    pallas_call x1, Pallas kernels: 120 us -> 115 us  [paired_body(): pl.pallas_call(paired_kernel, out_shape=jax.ShapeDtypeStruct((tok_dev, wi...]
where the time goes in v4:
time: 119 us
  Pallas kernels  115 us (97%)
  local copies, waits for them, and re-layouts  3.51 us (3%)
    pallas_call x1, Pallas kernels, paired_body(): pl.pallas_call(paired_kernel, out_shape=jax.ShapeDtypeStruct((tok_dev, wi...  115 us
    unnamed x5, local copies, waits for them, and re-layouts  3.51 us

profile of v4, /device:TPU:0, one launch (start us, length us, event | category | flops | bytes accessed | tf_op | source)
XLA Modules:
  0.0 118.8 jit_solution(2091273288124124230)
XLA Ops:
  0.0 0.8 copy.7.routes_ref
  0.8 0.8 copy.8.quanta_ref
  1.6 0.0 copy-start
  1.6 1.1 copy-done
  2.7 115.3 %shard_map.64 = bf16[128,2560]{1,0:T(8,128)(2,1)S(1)} custom-call(bf16[128,2560]{1,0:T(8,128)(2,1)S(1)} %copy-done, s32[128,6]{1,0:T(8,128)S(1)} %copy.7.routes_ref, s32[128,6]{1,0:T(8,128)S(1)} %copy.8.quanta_ref, bf16[1,2560,768]{2,1,0:T(8,128)(2,1)} %gw_hbm.1, bf16[1,2560,768]{2,1,0:T(8,128)(2,1)} %uw_hbm.1, bf16[1,768,2560]{2,1,0:T(8,128)(2,1)} %dw_hbm.1), custom_call_target="tpu_custom_call" | custom-call | flops 12079595520 | bytes 11796480 | tf_op jit(solution)/shard_map/pallas_call | solution.py:310
  118.0 0.8 copy.10
Async XLA Ops:
  1.6 1.1 copy-start

commit v5 on v4

--- a/solution.py
+++ b/solution.py
@@ -47,29 +47,28 @@
         )
     pl.semaphore_signal(barrier, inc=1, device_id=sibling, device_id_type=MESH)
 
-    lanes = lax.broadcasted_iota(jnp.int32, (tok_dev, 128), 1)
-    picked = jnp.zeros((tok_dev, 128), jnp.float32)
-    quanta = jnp.zeros((tok_dev, 128), jnp.int32)
-    for k in range(routes_ref.shape[1]):
-        route = routes_ref[:, k : k + 1]
-        picked += (route == lanes).astype(jnp.float32)
+    subs = lax.broadcasted_iota(jnp.int32, (EXTRA, tok_dev), 0)
+    picked = jnp.zeros((EXTRA, tok_dev), jnp.float32)
+    quanta = jnp.zeros((EXTRA, tok_dev), jnp.int32)
+    for k in range(routes_ref.shape[0]):
+        route = routes_ref[k : k + 1, :]
+        picked += (route == subs - 32).astype(jnp.float32)
         quanta += jnp.where(
-            (route == lanes) | (route == lanes - 16), quanta_ref[:, k : k + 1], 0
+            (route == subs) | (route == subs - 16), quanta_ref[k : k + 1, :], 0
         )
     upper = (quanta // 256).astype(jnp.float32) / 256.0
     lower = (quanta % 256).astype(jnp.float32) / 65536.0
-    before = (lax.broadcasted_iota(jnp.int32, (tok_dev, tok_dev), 1)
-              < lax.broadcasted_iota(jnp.int32, (tok_dev, tok_dev), 0))
+    before = (lax.broadcasted_iota(jnp.int32, (tok_dev, tok_dev), 0)
+              < lax.broadcasted_iota(jnp.int32, (tok_dev, tok_dev), 1))
     ranking = jnp.dot(
-        before.astype(jnp.bfloat16), picked.astype(jnp.bfloat16),
+        picked.astype(jnp.bfloat16), before.astype(jnp.bfloat16),
         preferred_element_type=jnp.float32,
     )
     slots = jnp.where(picked > 0.5, ranking, -1.0)
-    slot_t[0] = slots.T
+    marks = jnp.where(subs < 16, upper, jnp.where(subs < 32, lower, slots))
+    slot_t[0] = marks
     ext[0, :, :width] = tok_ref[...]
-    marks = jnp.where(lanes < 16, upper, lower)
-    ext[0, :, width : width + EXTRA] = marks.astype(jnp.bfloat16)
-    ext[0, :, width + EXTRA :] = slots.astype(jnp.bfloat16)
+    ext[0, :, width:] = marks.T.astype(jnp.bfloat16)
     slot_ids = lax.broadcasted_iota(jnp.int32, (cap, tok_dev), 0).astype(jnp.float32)
 
     pl.semaphore_wait(barrier, HALF + 1)
@@ -124,10 +123,10 @@
     def pick_rows(k):
         dest = flip(chip, lax.rem(k, HALF))
         held = k // HALF
-        chosen = (slot_t[held, pl.ds(2 * dest, 1), :] == slot_ids).astype(jnp.float32)
+        chosen = (slot_t[held, pl.ds(32 + 2 * dest, 1), :] == slot_ids).astype(jnp.float32)
         sel[k] = chosen
         return jnp.dot(
-            chosen.astype(jnp.bfloat16), ext[held, :, : width + EXTRA],
+            chosen.astype(jnp.bfloat16), ext[held],
             preferred_element_type=jnp.float32,
         ).astype(jnp.bfloat16)
 
@@ -219,7 +218,7 @@
         return carry
 
     block.wait_recv()
-    slot_t[1] = ext[1, :, width + EXTRA :].astype(jnp.float32).T
+    slot_t[1] = ext[1, :, width:].astype(jnp.float32).T
     lax.fori_loop(HALF + 1, CHIPS, dispatch, 0)
     recv[HALF, core] = pick_rows(HALF)
     share(HALF).start()
@@ -316,7 +315,7 @@
             pltpu.VMEM((width, hid), bf),
             pltpu.VMEM((width, hid), bf),
             pltpu.VMEM((hid, width), bf),
-            pltpu.VMEM((2, tok_dev, width + 2 * EXTRA), bf),
+            pltpu.VMEM((2, tok_dev, width + EXTRA), bf),
             pltpu.VMEM((2, 128, tok_dev), f32),
             pltpu.VMEM((CHIPS, cap, tok_dev), f32),
             pltpu.VMEM((CHIPS, cap, width + EXTRA), bf),
@@ -338,7 +337,7 @@
         cost_estimate=pl.CostEstimate(
             flops=6 * 16 * cap * width * hid, bytes_accessed=6 * width * hid, transcendentals=0
         ),
-    )(tokens, routes, gate_quanta, gate_weight, up_weight, down_weight)
+    )(tokens, routes.T, gate_quanta.T, gate_weight, up_weight, down_weight)
 
 
 def expert_apply(received, gate_weight, up_weight, down_weight):

time: 119 us -> 117 us (0.983)
    pallas_call x1, Pallas kernels: 115 us -> 114 us  [paired_body(): pl.pallas_call(paired_kernel, out_shape=jax.ShapeDtypeStruct((tok_dev, wi...]
    unnamed x5 -> x7, local copies, waits for them, and re-layouts: 3.51 us -> 3.3 us
where the time goes in v5:
time: 117 us
  Pallas kernels  114 us (97%)
  local copies, waits for them, and re-layouts  3.3 us (3%)
    pallas_call x1, Pallas kernels, paired_body(): pl.pallas_call(paired_kernel, out_shape=jax.ShapeDtypeStruct((tok_dev, wi...  114 us
    unnamed x7, local copies, waits for them, and re-layouts  3.3 us

profile of v5, /device:TPU:0, one launch (start us, length us, event | category | flops | bytes accessed | tf_op | source)
XLA Modules:
  0.0 117.2 jit_solution(8908354533059986731)
XLA Ops:
  0.0 0.0 copy-start
  0.0 1.1 copy-done
  1.1 0.0 copy-start.1
  1.1 0.7 copy-done.1
  1.8 0.0 copy-start.2
  1.8 0.7 copy-done.2
  2.5 113.9 %shard_map.64 = bf16[128,2560]{1,0:T(8,128)(2,1)S(1)} custom-call(bf16[128,2560]{1,0:T(8,128)(2,1)S(1)} %copy-done, s32[6,128]{1,0:T(8,128)S(1)} %bitcast.2, s32[6,128]{1,0:T(8,128)S(1)} %bitcast.3, bf16[1,2560,768]{2,1,0:T(8,128)(2,1)} %gw_hbm.1, bf16[1,2560,768]{2,1,0:T(8,128)(2,1)} %uw_hbm.1, bf16[1,768,2560]{2,1,0:T(8,128)(2,1)} %dw_hbm.1), custom_call_target="tpu_custom_call" | custom-call | flops 12079595520 | bytes 11796480 | tf_op jit(solution)/shard_map/pallas_call | solution.py:309
  116.3 0.8 copy.8
Async XLA Ops:
  0.0 1.1 copy-start
  1.1 0.7 copy-start.1
  1.8 0.7 copy-start.2

commit v6 on v5

--- a/solution.py
+++ b/solution.py
@@ -219,7 +219,7 @@
 
     block.wait_recv()
     slot_t[1] = ext[1, :, width:].astype(jnp.float32).T
-    lax.fori_loop(HALF + 1, CHIPS, dispatch, 0)
+    lax.fori_loop(HALF + 1, CHIPS, lambda k, c: dispatch(CHIPS + HALF - k, c), 0)
     recv[HALF, core] = pick_rows(HALF)
     share(HALF).start()
     for load in loads:

time: 117 us -> 115 us (0.983)
  Pallas kernels: 114 us -> 111 us
    pallas_call x1, Pallas kernels: 114 us -> 111 us  [paired_body(): pl.pallas_call(paired_kernel, out_shape=jax.ShapeDtypeStruct((tok_dev, wi...]
where the time goes in v6:
time: 115 us
  Pallas kernels  111 us (97%)
  local copies, waits for them, and re-layouts  3.3 us (3%)
    pallas_call x1, Pallas kernels, paired_body(): pl.pallas_call(paired_kernel, out_shape=jax.ShapeDtypeStruct((tok_dev, wi...  111 us
    unnamed x7, local copies, waits for them, and re-layouts  3.3 us

profile of v6, /device:TPU:0, one launch (start us, length us, event | category | flops | bytes accessed | tf_op | source)
XLA Modules:
  0.0 114.8 jit_solution(16538818043257879703)
XLA Ops:
  0.0 0.0 copy-start
  0.0 1.1 copy-done
  1.1 0.0 copy-start.1
  1.1 0.7 copy-done.1
  1.8 0.0 copy-start.2
  1.8 0.7 copy-done.2
  2.5 111.5 %shard_map.64 = bf16[128,2560]{1,0:T(8,128)(2,1)S(1)} custom-call(bf16[128,2560]{1,0:T(8,128)(2,1)S(1)} %copy-done, s32[6,128]{1,0:T(8,128)S(1)} %bitcast.2, s32[6,128]{1,0:T(8,128)S(1)} %bitcast.3, bf16[1,2560,768]{2,1,0:T(8,128)(2,1)} %gw_hbm.1, bf16[1,2560,768]{2,1,0:T(8,128)(2,1)} %uw_hbm.1, bf16[1,768,2560]{2,1,0:T(8,128)(2,1)} %dw_hbm.1), custom_call_target="tpu_custom_call" | custom-call | flops 12079595520 | bytes 11796480 | tf_op jit(solution)/shard_map/pallas_call | solution.py:309
  113.9 0.8 copy.8
Async XLA Ops:
  0.0 1.1 copy-start
  1.1 0.7 copy-start.1
  1.8 0.7 copy-start.2
